TPU v7x, 512 devices: a whole 4x4x16 slice. The times are simulated.
512 devices in a mesh: head: 4 (over x), vocab: 128 (over y, z, core).
Axes of the slice: x: 4, y: 4, z: 16, core: 2. Of those that a mesh axis runs over, the one named last changes fastest.
Arguments:
- hidden: bfloat16 [128, 4096], P(None, 'vocab'), may hold values from -6 to 6
- res_weight: bfloat16 [4, 4096, 4096], P('head', None, 'vocab'), may hold values from -0.09375 to 0.09375
- res_bias: float32 [4, 4096], P('head', 'vocab'), may hold values from -3 to 3
- out_weight: bfloat16 [4, 65536, 4096], P('head', 'vocab'), may hold values from -4 to 4
- targets: int32 [4, 128], P('head'), may hold values from 0 to 65535
- loss_mask: int32 [4, 128], P('head'), may hold values 0 or 1
Outputs:
- grad_hidden: float32 [128, 4096], P(None, 'vocab')
- grad_res_weight: float32 [4, 4096, 4096], P('head', None, 'vocab')
- grad_res_bias: float32 [4, 4096], P('head', 'vocab')
- head_loss: float32 [4], P('head')
All inputs are finite; a program needn't handle non-finite values. No bound on the sum of `loss_mask` on one device may be relied on, other than what follows from the above.
Results may differ from a plain program's by a relative error of at most 0.0075.
The roundings to bfloat16 on the way count: a program that leaves them out, or rounds other values in their place, can miss the bound.
Values may be sent and summed in bfloat16 or wider, within the bound.
A program may use at most 64 MiB of HBM per device.

v0:
```python
import jax
import jax.numpy as jnp
from jax import lax
from jax.sharding import PartitionSpec as P


def body(hidden, res_weight, res_bias, out_weight, targets, loss_mask):
    head_id = lax.axis_index("head")
    shard_id = lax.axis_index("vocab")
    rows = hidden.shape[0]
    vocab_rows = out_weight.shape[1]
    w_res = res_weight[0]
    w_out = out_weight[0]
    target = targets[0]
    full_rows = lax.all_gather(hidden, "vocab", axis=1, tiled=True)
    pre_t = (
        lax.dot_general(
            w_res, full_rows, (((0,), (1,)), ((), ())), preferred_element_type=jnp.float32
        )
        + res_bias[0][:, None]
    )
    block_t = (hidden.T.astype(jnp.float32) + jax.nn.silu(pre_t)).astype(jnp.bfloat16)
    block_full = lax.all_gather(block_t, "vocab", axis=0, tiled=True)
    logits = jnp.dot(w_out, block_full, preferred_element_type=jnp.float32)
    vocab_ids = shard_id * vocab_rows + lax.broadcasted_iota(jnp.int32, (vocab_rows, rows), 0)
    onehot = vocab_ids == target[None, :]
    local_picked = jnp.sum(jnp.where(onehot, logits, 0.0), axis=0)
    local_top = jnp.max(logits, axis=0)
    top = lax.pmax(local_top, "vocab")
    total, picked = lax.psum(
        (jnp.sum(jnp.exp(logits - top[None, :]), axis=0), local_picked), "vocab"
    )
    lse = top + jnp.log(total)
    factor = jnp.power(jnp.float32(0.8), (head_id + 1).astype(jnp.float32))
    row_weight = factor * loss_mask[0].astype(jnp.float32) / rows
    head_loss = jnp.sum(row_weight * (lse - picked)).reshape(1)
    dlogits = (
        row_weight[None, :] * (jnp.exp(logits - lse[None, :]) - onehot.astype(jnp.float32))
    ).astype(jnp.bfloat16)
    grad_block_t = lax.psum_scatter(
        lax.dot_general(
            w_out, dlogits, (((0,), (0,)), ((), ())), preferred_element_type=jnp.float32
        ),
        "vocab",
        scatter_dimension=0,
        tiled=True,
    )
    sig = jax.nn.sigmoid(pre_t)
    dpre_t = (grad_block_t * sig * (1.0 + pre_t * (1.0 - sig))).astype(jnp.bfloat16)
    grad_weight = lax.dot_general(
        full_rows, dpre_t, (((0,), (1,)), ((), ())), preferred_element_type=jnp.float32
    )
    grad_bias = jnp.sum(dpre_t.astype(jnp.float32), axis=1)
    partial_t = lax.psum_scatter(
        jnp.dot(w_res, dpre_t, preferred_element_type=jnp.float32),
        "vocab",
        scatter_dimension=0,
        tiled=True,
    )
    total_t = lax.psum(grad_block_t + partial_t, "head")
    return (total_t.T, grad_weight[None], grad_bias[None], head_loss)


def solution(mesh):
    placed = (
        P(None, "vocab"),
        P("head", None, "vocab"),
        P("head", "vocab"),
        P("head", "vocab", None),
        P("head", None),
        P("head", None),
    )
    return jax.shard_map(
        body,
        mesh=mesh,
        in_specs=placed,
        out_specs=(P(None, "vocab"), P("head", None, "vocab"), P("head", "vocab"), P("head")),
        check_vma=False,
    )
```

profile of v0, /device:TPU:1, one launch (start us, length us, event | category | flops | bytes accessed | tf_op | source)
XLA Modules:
  0.0 1308.7 jit_solution(1879619282172792385)
XLA Ops:
  7.2 0.0 copy-start
  7.2 0.0 copy-start.3
  7.2 0.0 copy-start.4
  7.2 0.0 all-gather.3.cloned.1.call-start
  7.2 0.7 all-gather.3.cloned.1.call-update
  7.9 0.0 all-gather.5.cloned.1.call-start
  8.0 139.4 %all-gather.3.cloned.1.call-done = bf16[128,4096]{0,1:T(8,128)(2,1)} async-done(((bf16[128,32]{0,1:T(8,128)(2,1)}), bf16[128,4096]{0,1:T(8,128)(2,1)}) %all-gather.3.cloned.1.call-update) | async-done | bytes 1048592 | tf_op jit(solution)/shard_map/all_gather | solution.py:15
  147.4 0.0 copy-done
  147.4 2.1 fusion.17
  149.6 0.0 all-gather.5.cloned.1.call-update
  149.6 0.0 reduce-scatter.3.cloned.1.call-start
  149.7 127.6 %all-gather.5.cloned.1.call-done = bf16[4096,128]{1,0:T(8,128)(2,1)} async-done(((bf16[32,128]{1,0:T(8,128)(2,1)}), bf16[4096,128]{1,0:T(8,128)(2,1)}) %all-gather.5.cloned.1.call-update) | async-done | bytes 1048592 | tf_op jit(solution)/shard_map/all_gather | solution.py:23
  277.4 4.1 fusion.18
  281.5 246.4 %pmax.7 = f32[128]{0:T(128)S(1)} all-reduce(f32[128]{0:T(128)S(1)} %get-tuple-element.15), channel_id=1, replica_groups=mesh['head'=4,'vocab'=128] {'vocab'}, use_global_device_ids=true, to_apply=%region_1.2 | all-reduce | flops 128 | bytes 1024 | tf_op jit(solution)/shard_map/pmax | solution.py:29
  527.9 0.0 copy-done.3
  527.9 0.2 fusion.6
  528.1 250.7 %all-reduce = (f32[128]{0:T(128)S(1)}, f32[128]{0:T(128)S(1)}) all-reduce(f32[128]{0:T(128)S(1)} %get-tuple-element.5, f32[128]{0:T(128)S(1)} %get-tuple-element.4), channel_id=1, replica_groups=mesh['head'=4,'vocab'=128] {'vocab'}, use_global_device_ids=true, to_apply=%region_3.4 | all-reduce | flops 256 | bytes 2048 | tf_op jit(solution)/shard_map/psum | solution.py:30
  778.8 0.0 copy-done.4
  778.8 0.6 multiply_reduce_fusion
  779.4 5.4 convolution_bitcast_fusion.1
  784.8 0.0 copy-start.1
  784.8 0.0 reduce-scatter.3.cloned.1.call-update
  784.8 0.0 reduce-scatter.5.cloned.1.call-start
  784.9 239.1 %reduce-scatter.3.cloned.1.call-done = f32[32,128]{1,0:T(8,128)} async-done(((f32[4096,128]{1,0:T(8,128)}), f32[32,128]{1,0:T(8,128)}) %reduce-scatter.3.cloned.1.call-update) | async-done | bytes 16400 | tf_op jit(solution)/shard_map/reduce_scatter | solution.py:40
  1024.0 0.0 copy-start.2
  1024.0 1.4 convert_reduce_fusion
  1025.4 1.9 convolution_bitcast_fusion
  1027.3 0.0 reduce-scatter.5.cloned.1.call-update
  1027.3 0.0 copy-done.1
  1027.3 1.3 convolution_bitcast_fusion.2
  1028.6 258.8 %reduce-scatter.5.cloned.1.call-done = f32[32,128]{1,0:T(8,128)} async-done(((f32[4096,128]{1,0:T(8,128)}), f32[32,128]{1,0:T(8,128)}) %reduce-scatter.5.cloned.1.call-update) | async-done | bytes 16400 | tf_op jit(solution)/shard_map/reduce_scatter | solution.py:54
  1287.4 0.0 copy-done.2
  1287.4 0.7 add_bitcast_fusion
  1288.1 14.1 %psum.22 = f32[128,32]{0,1:T(8,128)} all-reduce(f32[128,32]{0,1:T(8,128)S(1)} %add_bitcast_fusion), channel_id=1, replica_groups=mesh['head'=4,'vocab'=128] {'head'}, use_global_device_ids=true, to_apply=%region_6.7 | all-reduce | flops 4096 | bytes 32768 | tf_op jit(solution)/shard_map/psum | solution.py:60
  (1 shorter events, 0.0 us)
Async XLA Ops:
  7.2 140.3 %copy-start = (bf16[1,4096,32]{1,2,0:T(8,128)(2,1)S(1)}, bf16[1,4096,32]{1,2,0:T(8,128)(2,1)}, u32[]{:S(2)}) copy-start(bf16[1,4096,32]{1,2,0:T(8,128)(2,1)} %param.7) | copy-start | bytes 786436
  7.2 520.7 %copy-start.3 = (s32[1,128]{1,0:T(1,128)S(1)}, s32[1,128]{1,0:T(1,128)}, u32[]{:S(2)}) copy-start(s32[1,128]{1,0:T(1,128)} %param.10) | copy-start | bytes 1540
  7.2 771.6 %copy-start.4 = (s32[1,128]{1,0:T(1,128)S(1)}, s32[1,128]{1,0:T(1,128)}, u32[]{:S(2)}) copy-start(s32[1,128]{1,0:T(1,128)} %param.11) | copy-start | bytes 1540
  7.2 140.2 %all-gather.3.cloned.1.call-start = ((), (), s32[]{:S(2)}) async-start(), calls=%async_computation.2 | async-start | bytes 1056768 | tf_op jit(solution)/shard_map/all_gather | solution.py:15
  7.9 269.4 %all-gather.5.cloned.1.call-start = ((), (), s32[]{:S(2)}) async-start(), calls=%async_computation.3 | async-start | bytes 1056768 | tf_op jit(solution)/shard_map/all_gather | solution.py:23
  149.6 874.4 %reduce-scatter.3.cloned.1.call-start = ((), (), s32[]{:S(2)}) async-start(), calls=%async_computation.4 | async-start | bytes 2113536 | tf_op jit(solution)/shard_map/reduce_scatter | solution.py:40
  784.8 242.5 %copy-start.1 = (bf16[128,4096]{0,1:T(8,128)(2,1)S(1)}, bf16[128,4096]{0,1:T(8,128)(2,1)}, u32[]{:S(2)}) copy-start(bf16[128,4096]{0,1:T(8,128)(2,1)} %all-gather.3.cloned.1.call-done) | copy-start | bytes 3145732
  784.8 502.6 %reduce-scatter.5.cloned.1.call-start = ((), (), s32[]{:S(2)}) async-start(), calls=%async_computation.5 | async-start | bytes 2113536 | tf_op jit(solution)/shard_map/reduce_scatter | solution.py:54
  1024.0 263.4 %copy-start.2 = (f32[32,128]{1,0:T(8,128)S(1)}, f32[32,128]{1,0:T(8,128)}, u32[]{:S(2)}) copy-start(f32[32,128]{1,0:T(8,128)} %reduce-scatter.3.cloned.1.call-done) | copy-start | bytes 49156
Sparse Core Ops, SparseCore 0:
  11.0 136.3 all-gather.2
  151.0 126.3 all-gather.4
  785.0 238.9 reduce-scatter.2
  1028.4 258.9 reduce-scatter.4
where the time goes:
time: 1320 us; the launch traced here: 1310 us
  waiting for transfers between devices  766 us (58%)
  blocking collectives  511 us (39%)
  matrix products  14.7 us (1%)
  between operations  13.9 us (1%)
    reduce_scatter x1, waiting for transfers between devices, body(): lax.psum_scatter(jnp.dot(w_res, dpre_t, preferred_element_type=jnp.float3...  259 us
    psum x1, blocking collectives, body(): lax.psum((jnp.sum(jnp.exp(logits - top[None, :]), axis=0), local_picked),...  251 us
    pmax x1, blocking collectives, body(): top = lax.pmax(local_top, 'vocab')  246 us
    reduce_scatter x1, waiting for transfers between devices, body(): lax.psum_scatter(lax.dot_general(w_out, dlogits, (((0,), (0,)), ((), ()))...  239 us
    all_gather x1, waiting for transfers between devices, body(): full_rows = lax.all_gather(hidden, 'vocab', axis=1, tiled=True)  139 us
    all_gather x1, waiting for transfers between devices, body(): block_full = lax.all_gather(block_t, 'vocab', axis=0, tiled=True)  128 us
  transfers between devices with their start and end apart: 4, of which 4 were waited for; matrix products, arithmetic and copies ran while one was open for 0% of the time, Pallas kernels for 0%

commit v1 on v0

v1 whole, which is shorter than its diff:
```python
import functools

import jax
import jax.numpy as jnp
from jax import lax
from jax.experimental import pallas as pl
from jax.experimental.pallas import tpu as pltpu
from jax.sharding import PartitionSpec as P

MESH = pl.DeviceIdType.MESH
F32, BF16 = jnp.float32, jnp.bfloat16
GRID = {128: (4, 16), 16: (2, 4), 8: (2, 2)}
FEAT = 32
PARTS = 4


class Place:
    def __init__(self, heads, vocab):
        self.heads = heads
        self.ny, self.nz = GRID[vocab]
        v = lax.axis_index("vocab")
        self.x = lax.axis_index("head")
        self.v = v
        self.y = lax.div(v, 2 * self.nz)
        self.z = lax.rem(lax.div(v, 2), self.nz)
        self.c = lax.rem(v, 2)
        half = self.nz // 2
        self.dist = sorted(range(self.nz), key=lambda d: (-min(d, self.nz - d), d))
        self.slot_of = {d: j for j, d in enumerate(self.dist)}
        self.half = half
        self.parts = min(PARTS, self.nz)
        self.gs = self.nz // self.parts
        self.ydist = sorted(range(1, self.ny), key=lambda d: (-min(d, self.ny - d), d))

    def slot(self, z_abs):
        d = lax.rem(z_abs - self.z + self.nz, self.nz)
        return jnp.where(d >= self.half, jnp.where(d == self.half, 0, 2 * (d - self.half)), 2 * (self.half - d) - 1)

    def yat(self, d):
        return lax.rem(self.y + d + self.ny, self.ny)

    def zat(self, d):
        return lax.rem(self.z + d + self.nz, self.nz)

    def dev(self, y, z, c):
        return (self.x, (y * self.nz + z) * 2 + c)


def remote(src, dst, send, recv, dev):
    return pltpu.make_async_remote_copy(
        src_ref=src, dst_ref=dst, send_sem=send, recv_sem=recv, device_id=dev, device_id_type=MESH
    )


def gather(pt, buf, sems, sent):
    zs, zr, ys, yr, cs, cr = sems
    own = pt.nz - 1
    sib = pt.dev(pt.y, pt.z, 1 - pt.c)
    arrive_z = {}
    for j, d in enumerate(pt.dist[:-1]):
        there = pt.slot_of[(pt.nz - d) % pt.nz]
        cp = remote(
            buf.at[pt.c, pt.y, own], buf.at[pt.c, pt.y, there], zs.at[j], zr.at[there], pt.dev(pt.y, pt.zat(d), pt.c)
        )
        cp.start()
        sent.append(cp)
        arrive_z[there] = cp

    def group(core, y, g):
        return buf.at[core, y, pl.ds(g * pt.gs, pt.gs)]

    def across(p, y, g):
        cp = remote(group(pt.c, y, g), group(pt.c, y, g), cs.at[p, g], cr.at[p, g], sib)
        cp.start()
        sent.append(cp)

    def pass_on(g):
        for d in reversed(pt.ydist):
            y = pt.yat(-d)
            remote(group(pt.c, y, g), group(pt.c, y, g), ys.at[d - 1, g], yr.at[d - 1, g], sib).wait_recv()
            across(d, y, g)

    for g in reversed(range(pt.parts)):
        for j in range(g * pt.gs, (g + 1) * pt.gs):
            if j != own:
                arrive_z[j].wait_recv()
        for d in pt.ydist:
            cp = remote(
                group(pt.c, pt.y, g),
                group(pt.c, pt.y, g),
                ys.at[d - 1, g],
                yr.at[d - 1, g],
                pt.dev(pt.yat(d), pt.z, pt.c),
            )
            cp.start()
            sent.append(cp)
        across(0, pt.y, g)
        if g + 1 < pt.parts:
            pass_on(g + 1)
    pass_on(0)
    for g in reversed(range(pt.parts)):
        for p in range(pt.ny):
            y = pt.yat(-p)
            remote(group(1 - pt.c, y, g), group(1 - pt.c, y, g), cs.at[p, g], cr.at[p, g], sib).wait_recv()


def in_order(pt, buf, flat):
    def step(i, carry):
        y, z = lax.div(i, pt.nz), lax.rem(i, pt.nz)
        j = pt.slot(z)
        for core in range(2):
            flat[pl.ds(pl.multiple_of((i * 2 + core) * FEAT, FEAT), FEAT), :] = buf[core, y, j]
        return carry

    lax.fori_loop(0, pt.ny * pt.nz, step, 0, unroll=4)


def scatter(pt, theirs, mine, bufs, sems, sent, between=None):
    to_core, from_core, to_y, from_y, to_z, from_z = bufs
    cs, cr, ys, yr, zs, zr = sems
    sib = pt.dev(pt.y, pt.z, 1 - pt.c)
    n = pt.gs * FEAT
    last = pt.parts - 1

    def rows(g):
        return pl.ds(g * n, n)

    order = pt.ydist + [0]
    core_copies = {}
    for d in order:
        y = pt.yat(d)
        for g in range(pt.parts):
            to_core[d, rows(g), :] = theirs(y, g).astype(BF16)
        cp = remote(to_core.at[d], from_core.at[d], cs.at[d], cr.at[d], sib)
        cp.start()
        sent.append(cp)
        core_copies[d] = cp
    y_copies = {}
    for g in range(pt.parts):
        for d in pt.ydist:
            y = pt.yat(d)
            if g == 0:
                core_copies[d].wait_recv()
            to_y[d - 1, rows(g), :] = (mine(y, g) + from_core[d, rows(g), :].astype(F32)).astype(BF16)
            cp = remote(
                to_y.at[d - 1, rows(g)],
                from_y.at[d - 1, rows(g)],
                ys.at[d - 1, g],
                yr.at[d - 1, g],
                pt.dev(y, pt.z, pt.c),
            )
            cp.start()
            sent.append(cp)
            y_copies[d, g] = cp
    core_copies[0].wait_recv()
    if between is not None:
        between()
    total = None
    z_copies = []
    for g in range(pt.parts):
        acc = mine(pt.y, g) + from_core[0, rows(g), :].astype(F32)
        for d in reversed(pt.ydist):
            y_copies[d, g].wait_recv()
            acc = acc + from_y[d - 1, rows(g), :].astype(F32)
        to_z[rows(g), :] = acc.astype(BF16)
        if g == last:
            total = acc[n - FEAT :, :]
        for j in range(g * pt.gs, (g + 1) * pt.gs):
            if j == pt.nz - 1:
                continue
            d = pt.dist[j]
            there = pt.slot_of[(pt.nz - d) % pt.nz]
            cp = remote(
                to_z.at[pl.ds(j * FEAT, FEAT)],
                from_z.at[there],
                zs.at[j],
                zr.at[there],
                pt.dev(pt.y, pt.zat(d), pt.c),
            )
            cp.start()
            sent.append(cp)
            z_copies.append((there, cp))
    for there, cp in sorted(z_copies, key=lambda t: -t[0]):
        cp.wait_recv()
        total = total + from_z[there].astype(F32)
    return total


def kernel(heads, vocab, *refs):
    (hid, bias, tgt, msk, wres_hbm, wout_hbm, gh_out, gw_out, gb_out, loss_out) = refs[:10]
    (wo, wot, wr, wrt, buf1, buf2, flat1, flat2, logits, eo, prod, prod2, gw, st, st_y, sz, st_z, gx, gx_in) = refs[10:29]
    rs1, rs2 = refs[29:35], refs[35:41]
    ag1_s, ag2_s, rs1_s, rs2_s = refs[41:47], refs[47:53], refs[53:59], refs[59:65]
    sys_, syr, szs, szr, xs, xr, local = refs[65:72]
    pt = Place(heads, vocab)
    ny, nz = pt.ny, pt.nz
    nrow = hid.shape[1]
    nvoc = wo.shape[0]
    feats = wo.shape[1]
    ychunk = feats // ny
    sent = []

    get_wr = pltpu.make_async_copy(wres_hbm, wr, local.at[0])
    get_wo = pltpu.make_async_copy(wout_hbm, wo, local.at[1])
    get_wr.start()
    get_wo.start()

    peers = [pt.dev(pt.y, pt.zat(d), pt.c) for d in pt.dist[:-1]]
    plane = [(dy, dc) for dy in range(ny) for dc in range(2) if dy or dc]
    near = [pt.dev(pt.yat(dy), pt.z, lax.rem(pt.c + dc, 2)) for dy, dc in plane]
    xpeers = [(lax.rem(pt.x + d, heads), pt.v) for d in range(1, heads)]
    barrier = pltpu.get_barrier_semaphore()
    for dev in peers + near + xpeers:
        pl.semaphore_signal(barrier, inc=1, device_id=dev, device_id_type=MESH)
    buf1[pt.c, pt.y, nz - 1] = hid[...]

    per = 256 // (2 * FEAT)

    def place_rows(dst, chunk, i):
        y = lax.div(i * per, nz)
        z0 = lax.rem(i * per, nz)
        for k in range(per):
            j = pt.slot(z0 + k)
            for core in range(2):
                r = (k * 2 + core) * FEAT
                dst[core, y, j] = chunk[r : r + FEAT, :]

    def turn_wr(i, carry):
        place_rows(wrt, wr[:, pl.ds(pl.multiple_of(i * 256, 256), 256)].T, i)
        return carry

    get_wr.wait()
    lax.fori_loop(0, feats // 256, turn_wr, 0)
    pl.semaphore_wait(barrier, len(peers) + len(near) + len(xpeers))

    def turn_wo(i, carry):
        place_rows(wot, wo[:, pl.ds(pl.multiple_of(i * 256, 256), 256)].T, i)
        return carry

    gather(pt, buf1, ag1_s, sent)
    in_order(pt, buf1, flat1)

    eye = lax.broadcasted_iota(jnp.int32, (FEAT, FEAT), 0) == lax.broadcasted_iota(jnp.int32, (FEAT, FEAT), 1)
    bias_col = jnp.sum(jnp.where(eye, bias[...], 0.0), axis=1, keepdims=True)
    pre = jnp.zeros((FEAT, nrow), F32)
    for y in range(ny):
        pre = pre + jnp.dot(
            wr[:, y * ychunk : (y + 1) * ychunk], flat1[y * ychunk : (y + 1) * ychunk, :], preferred_element_type=F32
        )
    pre = pre + bias_col
    sig = jax.nn.sigmoid(pre)
    buf2[pt.c, pt.y, nz - 1] = (hid[...].astype(F32) + pre * sig).astype(BF16)
    gate = sig * (1.0 + pre * (1.0 - sig))

    get_wo.wait()
    lax.fori_loop(0, feats // 256, turn_wo, 0)
    gather(pt, buf2, ag2_s, sent)
    in_order(pt, buf2, flat2)

    logits[...] = jnp.zeros_like(logits)

    def logit_step(i, carry):
        at = pl.ds(pl.multiple_of(i * ychunk, ychunk), ychunk)
        logits[...] += jnp.dot(wo[:, at], flat2[at, :], preferred_element_type=F32)
        return carry

    lax.fori_loop(0, ny, logit_step, 0)
    ids = pt.v * nvoc + lax.broadcasted_iota(jnp.int32, (nvoc, nrow), 0)
    hit = ids == tgt[...]
    lg = logits[...]
    top = jnp.max(lg, axis=0, keepdims=True)
    picked = jnp.sum(jnp.where(hit, lg, 0.0), axis=0, keepdims=True)
    owned = jnp.sum(hit.astype(F32), axis=0, keepdims=True)
    e = jnp.exp(lg - top)
    tot = jnp.sum(e, axis=0, keepdims=True)
    eo[:, :nrow] = jnp.where(hit, 0.0, e).astype(BF16)
    eo[:, nrow:] = hit.astype(BF16)

    def pack(a, b, c):
        r = lax.broadcasted_iota(jnp.int32, (8, nrow), 0)
        return jnp.where(r == 0, a, jnp.where(r == 1, b, jnp.where(r == 2, c, 0.0)))

    def merge(ref, count):
        tops = [ref[i, 0:1, :] for i in range(count)]
        best = functools.reduce(jnp.maximum, tops)
        total = sum(ref[i, 1:2, :] * jnp.exp(tops[i] - best) for i in range(count))
        pick = sum(ref[i, 2:3, :] for i in range(count))
        return best, total, pick

    mine = pack(top, tot, picked)
    st[...] = mine
    me = pt.y * 2 + pt.c
    st_y[me] = mine
    y_copies = []
    for k, dev in enumerate(near):
        cp = remote(st, st_y.at[me], sys_.at[k], syr.at[k], dev)
        cp.start()
        sent.append(cp)
        y_copies.append(cp)

    def product(i, carry):
        core, y = lax.div(i, ny), lax.rem(i, ny)
        prod[core, y] = jnp.dot(
            wot[core, y].reshape(nz * FEAT, nvoc), eo[...], preferred_element_type=F32
        )
        return carry

    lax.fori_loop(0, ny, product, 0)
    for cp in y_copies:
        cp.wait_recv()
    mine = pack(*merge(st_y, ny * 2))
    sz[...] = mine
    st_z[pt.z] = mine
    z_copies = []
    for j, d in enumerate(pt.dist[:-1]):
        cp = remote(sz, st_z.at[pt.z], szs.at[j], szr.at[j], pt.dev(pt.y, pt.zat(d), pt.c))
        cp.start()
        sent.append(cp)
        z_copies.append(cp)
    lax.fori_loop(ny, 2 * ny, product, 0)
    for cp in z_copies:
        cp.wait_recv()
    best, total, pick = merge(st_z, nz)
    lse = best + jnp.log(total)
    factor = jnp.float32(0.8 ** heads)
    for k in range(heads - 1):
        factor = jnp.where(pt.x == k, jnp.float32(0.8 ** (k + 1)), factor)
    weight = factor * msk[...].astype(F32) / nrow
    loss_out[...] = jnp.sum(weight * (lse - pick), axis=1, keepdims=True)
    alpha = weight * jnp.exp(top - lse)
    beta = jnp.where(owned > 0.0, weight * (jnp.exp(picked - lse) - 1.0), 0.0).astype(BF16).astype(F32)

    n = pt.gs * FEAT

    def term(core, y, g):
        return alpha * prod[core, y, g * n : (g + 1) * n, :nrow] + beta * prod[core, y, g * n : (g + 1) * n, nrow:]

    dh = scatter(
        pt, lambda y, g: term(1 - pt.c, y, g), lambda y, g: term(pt.c, y, g), rs1, rs1_s, sent
    )
    dpre = (dh * gate).astype(BF16)
    gb = jnp.sum(dpre.astype(F32), axis=1, keepdims=True)
    gb_out[...] = jnp.sum(jnp.where(eye, gb, 0.0), axis=0, keepdims=True)

    for core in range(2):
        for y in range(ny):
            prod2[core, y] = jnp.dot(
                wrt[core, y].reshape(nz * FEAT, FEAT), dpre, preferred_element_type=F32
            )
    put_gw = pltpu.make_async_copy(gw, gw_out, local.at[2])

    def weight_grad():
        def step(i, carry):
            at = pl.ds(pl.multiple_of(i * 256, 256), 256)
            gw[:, at] = lax.dot_general(
                dpre, flat1[at, :], (((1,), (1,)), ((), ())), preferred_element_type=F32
            )
            return carry

        lax.fori_loop(0, feats // 256, step, 0)
        put_gw.start()

    back = scatter(
        pt,
        lambda y, g: prod2[1 - pt.c, y, g * n : (g + 1) * n, :],
        lambda y, g: prod2[pt.c, y, g * n : (g + 1) * n, :],
        rs2,
        rs2_s,
        sent,
        weight_grad,
    )
    part = dh + back
    gx[...] = part
    gx_in[pt.x] = part
    x_copies = []
    for k, dev in enumerate(xpeers):
        cp = remote(gx, gx_in.at[pt.x], xs.at[k], xr.at[k], dev)
        cp.start()
        sent.append(cp)
        x_copies.append(cp)
    for cp in x_copies:
        cp.wait_recv()
    gh_out[...] = sum(gx_in[k] for k in range(heads))
    for cp in sent:
        cp.wait_send()
    put_gw.wait()


def body(heads, vocab, hidden, res_weight, res_bias, out_weight, targets, loss_mask):
    ny, nz = GRID[vocab]
    rows = hidden.shape[0]
    nvoc, feats = out_weight.shape[1:]
    parts = min(PARTS, nz)
    dma = pltpu.SemaphoreType.DMA
    vm = pltpu.VMEM
    gather_sems = [dma((nz,)), dma((nz,)), dma((ny, parts)), dma((ny, parts)), dma((ny, parts)), dma((ny, parts))]
    scatter_sems = [dma((ny,)), dma((ny,)), dma((ny, parts)), dma((ny, parts)), dma((nz,)), dma((nz,))]
    scatter_bufs = [
        vm((ny, nz * FEAT, rows), BF16),
        vm((ny, nz * FEAT, rows), BF16),
        vm((ny - 1, nz * FEAT, rows), BF16),
        vm((ny - 1, nz * FEAT, rows), BF16),
        vm((nz * FEAT, rows), BF16),
        vm((nz, FEAT, rows), BF16),
    ]
    in_vmem = pl.BlockSpec(memory_space=pltpu.VMEM)
    anywhere = pl.BlockSpec(memory_space=pl.ANY)
    gh, gw, gb, loss = pl.pallas_call(
        functools.partial(kernel, heads, vocab),
        out_shape=(
            jax.ShapeDtypeStruct((FEAT, rows), F32),
            jax.ShapeDtypeStruct((FEAT, feats), F32),
            jax.ShapeDtypeStruct((1, FEAT), F32),
            jax.ShapeDtypeStruct((1, 1), F32),
        ),
        in_specs=[in_vmem] * 4 + [anywhere] * 2,
        out_specs=(in_vmem, anywhere, in_vmem, in_vmem),
        scratch_shapes=[
            vm((nvoc, feats), BF16),
            vm((2, ny, nz, FEAT, nvoc), BF16),
            vm((FEAT, feats), BF16),
            vm((2, ny, nz, FEAT, FEAT), BF16),
            vm((2, ny, nz, FEAT, rows), BF16),
            vm((2, ny, nz, FEAT, rows), BF16),
            vm((feats, rows), BF16),
            vm((feats, rows), BF16),
            vm((nvoc, rows), F32),
            vm((nvoc, 2 * rows), BF16),
            vm((2, ny, nz * FEAT, 2 * rows), F32),
            vm((2, ny, nz * FEAT, rows), F32),
            vm((FEAT, feats), F32),
            vm((8, rows), F32),
            vm((2 * ny, 8, rows), F32),
            vm((8, rows), F32),
            vm((nz, 8, rows), F32),
            vm((FEAT, rows), F32),
            vm((heads, FEAT, rows), F32),
            *scatter_bufs,
            *scatter_bufs,
            *gather_sems,
            *gather_sems,
            *scatter_sems,
            *scatter_sems,
            dma((2 * ny,)),
            dma((2 * ny,)),
            dma((nz,)),
            dma((nz,)),
            dma((max(heads - 1, 1),)),
            dma((max(heads - 1, 1),)),
            dma((3,)),
        ],
        name="heads_backward",
        compiler_params=pltpu.CompilerParams(
            collective_id=0, has_side_effects=True, vmem_limit_bytes=48 << 20
        ),
    )(hidden.T, res_bias, targets, loss_mask, res_weight[0].T, out_weight[0])
    return gh.T, gw.T[None], gb, loss.reshape(1)


def solution(mesh):
    placed = (
        P(None, "vocab"),
        P("head", None, "vocab"),
        P("head", "vocab"),
        P("head", "vocab", None),
        P("head", None),
        P("head", None),
    )
    return jax.shard_map(
        functools.partial(body, mesh.shape["head"], mesh.shape["vocab"]),
        mesh=mesh,
        in_specs=placed,
        out_specs=(P(None, "vocab"), P("head", None, "vocab"), P("head", "vocab"), P("head")),
        check_vma=False,
    )
```

time: 1320 us -> 116 us (0.09)
  waiting for transfers between devices: 766 us -> 0 us
  blocking collectives: 511 us -> 0 us
  Pallas kernels: 0 us -> 105 us
  matrix products: 14.7 us -> 0 us
    reduce_scatter x2 -> x0, waiting for transfers between devices: 498 us -> none  [the longest x1 259 us: body(): lax.psum_scatter(jnp.dot(w_res, dpre_t, preferred_element_type=jnp.float3...]
    all_gather x2 -> x0, waiting for transfers between devices: 267 us -> none  [the longest x1 139 us: body(): full_rows = lax.all_gather(hidden, 'vocab', axis=1, tiled=True)]
    psum x2 -> x0, blocking collectives: 265 us -> none  [the longest x1 251 us: body(): lax.psum((jnp.sum(jnp.exp(logits - top[None, :]), axis=0), local_picked),...]
    pmax x1 -> x0, blocking collectives: 246 us -> none  [body(): top = lax.pmax(local_top, 'vocab')]
    pallas_call x0 -> x1, Pallas kernels: none -> 105 us  [body(): pl.pallas_call(functools.partial(kernel, heads, vocab), out_shape=(jax.Sh...]
    dot_general x5 -> x0, matrix products: 14.7 us -> none  [the longest x1 5.37 us: body(): lax.dot_general(w_out, dlogits, (((0,), (0,)), ((), ())), preferred_eleme...]
  transfers between devices with their start and end apart: 4 -> 0, of which waited for: 4 -> 0; matrix products, arithmetic and copies ran while one was open for 0% -> 0% of each run, Pallas kernels for 0% -> 0%
where the time goes in v1:
time: 116 us; the launch traced here: 115 us
  Pallas kernels  105 us (91%)
  local copies, waits for them, and re-layouts  7.7 us (7%)
  between operations  2.47 us (2%)
    pallas_call x1, Pallas kernels, body(): pl.pallas_call(functools.partial(kernel, heads, vocab), out_shape=(jax.Sh...  105 us
    unnamed x15, local copies, waits for them, and re-layouts  7.7 us

profile of v1, /device:TPU:1, one launch (start us, length us, event | category | flops | bytes accessed | tf_op | source)
XLA Modules:
  0.0 115.1 jit_solution(5203293841158137594)
XLA Ops:
  0.6 0.0 copy-start
  0.6 2.2 %copy-done = bf16[1,512,4096]{2,1,0:T(8,128)(2,1)S(1)} copy-done((bf16[1,512,4096]{2,1,0:T(8,128)(2,1)S(1)}, bf16[1,512,4096]{2,1,0:T(8,128)(2,1)}, u32[]{:S(2)}) %copy-start) | copy-done | bytes 4194328
  2.8 0.0 copy-start.1
  2.8 0.9 copy-done.1
  3.8 0.0 copy-start.2
  3.8 0.7 copy-done.2
  4.5 0.0 copy-start.3
  4.5 0.7 copy-done.3
  5.1 0.0 copy-start.4
  5.1 0.7 copy-done.4
  5.8 0.0 copy-start.5
  5.8 0.7 copy-done.5
  6.4 104.9 %heads_backward.1 = (f32[32,128]{1,0:T(8,128)S(1)}, f32[32,4096]{1,0:T(8,128)S(1)}, f32[1,32]{1,0:T(1,128)S(1)}, f32[1,1]{1,0:T(1,128)}) custom-call(bf16[32,128]{1,0:T(8,128)(2,1)S(1)} %bitcast.14, f32[1,32]{1,0:T(1,128)S(1)} %copy-done.3, s32[1,128]{1,0:T(1,128)S(1)} %copy-done.4, s32[1,128]{1,0:T(1,128)S(1)} %copy-done.5, bf16[32,4096]{1,0:T(8,128)(2,1)S(1)} %bitcast.12, ...), custom_call_target="tpu_custom_call" | custom-call | tf_op jit(solution)/shard_map/heads_backward/pallas_call | solution.py:408
  111.3 0.6 copy.14
  111.9 0.8 copy.15
  112.7 0.5 copy.16
Async XLA Ops:
  0.6 2.2 %copy-start = (bf16[1,512,4096]{2,1,0:T(8,128)(2,1)S(1)}, bf16[1,512,4096]{2,1,0:T(8,128)(2,1)}, u32[]{:S(2)}) copy-start(bf16[1,512,4096]{2,1,0:T(8,128)(2,1)} %param.9) | copy-start | bytes 12582916
  2.8 0.9 copy-start.1
  3.8 0.7 copy-start.2
  4.5 0.7 copy-start.3
  5.1 0.7 copy-start.4
  5.8 0.7 copy-start.5

commit v2 on v1

v2 whole, which is shorter than its diff:
```python
import functools

import jax
import jax.numpy as jnp
from jax import lax
from jax.experimental import pallas as pl
from jax.experimental.pallas import tpu as pltpu
from jax.sharding import PartitionSpec as P

MESH = pl.DeviceIdType.MESH
F32, BF16 = jnp.float32, jnp.bfloat16
GRID = {128: (4, 16), 16: (2, 4), 8: (2, 2)}
FEAT = 32
PARTS = 4
NEAR = 8


class Place:
    def __init__(self, heads, vocab):
        self.heads = heads
        self.ny, self.nz = GRID[vocab]
        v = lax.axis_index("vocab")
        self.x = lax.axis_index("head")
        self.v = v
        self.y = lax.div(v, 2 * self.nz)
        self.z = lax.rem(lax.div(v, 2), self.nz)
        self.c = lax.rem(v, 2)
        half = self.nz // 2
        self.dist = sorted(range(self.nz), key=lambda d: (-min(d, self.nz - d), d))
        self.slot_of = {d: j for j, d in enumerate(self.dist)}
        self.half = half
        self.parts = min(PARTS, self.nz)
        self.gs = self.nz // self.parts
        self.near = min(NEAR, self.nz // 2)
        self.sib = (self.x, v + 1 - 2 * self.c)
        self.ydist = sorted(range(1, self.ny), key=lambda d: (-min(d, self.ny - d), d))

    def slot(self, z_abs):
        d = lax.rem(z_abs - self.z + self.nz, self.nz)
        return jnp.where(d >= self.half, jnp.where(d == self.half, 0, 2 * (d - self.half)), 2 * (self.half - d) - 1)

    def yat(self, d):
        return lax.rem(self.y + d + self.ny, self.ny)

    def zat(self, d):
        return lax.rem(self.z + d + self.nz, self.nz)

    def dev(self, y, z, c):
        return (self.x, (y * self.nz + z) * 2 + c)


def remote(src, dst, send, recv, dev):
    return pltpu.make_async_remote_copy(
        src_ref=src, dst_ref=dst, send_sem=send, recv_sem=recv, device_id=dev, device_id_type=MESH
    )


class Sends:
    def __init__(self, pt):
        self.pt = pt
        self.open = []

    def add(self, ref, sem):
        self.open.append((ref, sem))

    def flush(self):
        for ref, sem in self.open:
            remote(ref, ref, sem, sem, self.pt.sib).wait_send()
        self.open = []


def arrived(pt, ref, sem):
    remote(ref, ref, sem, sem, pt.sib).wait_recv()


def gather(pt, buf, sems, sends, between=None):
    zs, ys, cs, cr = (sems.at[k] for k in range(4))
    own = pt.nz - 1
    c = pt.c
    groups = ((pt.nz - pt.near, pt.nz), (0, pt.nz - pt.near))
    for d in pt.dist[:-1]:
        there = pt.slot_of[(pt.nz - d) % pt.nz]
        g = 0 if there >= groups[0][0] else 1
        remote(buf.at[c, 0, own], buf.at[c, 0, there], zs, sems.at[4 + g], pt.dev(pt.y, pt.zat(d), c)).start()
    if between is not None:
        between()

    def across(rows, lo, hi):
        part = buf.at[c, pl.ds(*rows), pl.ds(lo, hi - lo)]
        remote(part, part, cs, cr, pt.sib).start()

    for g, (lo, hi) in enumerate(groups):
        n = hi - lo - (g == 0)
        arrived(pt, buf.at[c, 0, pl.ds(lo, n)], sems.at[4 + g])
        for d in pt.ydist:
            remote(
                buf.at[c, 0, pl.ds(lo, hi - lo)],
                buf.at[c, d, pl.ds(lo, hi - lo)],
                ys,
                sems.at[6 + g],
                pt.dev(pt.yat(d), pt.z, c),
            ).start()
        across((0, 1), lo, hi)
    for g, (lo, hi) in enumerate(groups):
        arrived(pt, buf.at[c, pl.ds(1, pt.ny - 1), pl.ds(lo, hi - lo)], sems.at[6 + g])
        across((1, pt.ny - 1), lo, hi)
    arrived(pt, buf.at[1 - c], cr)
    sends.add(buf.at[c, 0, pl.ds(0, own)], zs)
    sends.add(buf.at[c, pl.ds(1, pt.ny - 1)], ys)
    sends.add(buf.at[c], cs)


def in_order(pt, buf, flat):
    def step(i, carry):
        y, z = lax.div(i, pt.nz), lax.rem(i, pt.nz)
        j = pt.slot(z)
        y = lax.rem(pt.y - y + pt.ny, pt.ny)
        for core in range(2):
            flat[pl.ds(pl.multiple_of((i * 2 + core) * FEAT, FEAT), FEAT), :] = buf[core, y, j]
        return carry

    lax.fori_loop(0, pt.ny * pt.nz, step, 0, unroll=4)


def scatter(pt, theirs, mine, bufs, sems, sends, beside=None, between=None, finish=None):
    to_core, from_core, to_y, from_y, to_z, from_z = bufs
    cs, ys, zs, zr = (sems.at[k] for k in range(4))
    n = pt.gs * FEAT
    last = pt.parts - 1

    def rows(g):
        return pl.ds(g * n, n)

    for d in pt.ydist + [0]:
        for g in range(pt.parts):
            to_core[d, rows(g), :] = theirs(pt.yat(d), g).astype(BF16)
        remote(to_core.at[d], from_core.at[d], cs, sems.at[4 + d], pt.sib).start()
    sends.flush()
    sends.add(to_core, cs)
    if beside is not None:
        beside()
    for g in range(pt.parts):
        for d in pt.ydist:
            if g == 0:
                arrived(pt, from_core.at[d], sems.at[4 + d])
            to_y[d - 1, rows(g), :] = (mine(pt.yat(d), g) + from_core[d, rows(g), :].astype(F32)).astype(BF16)
            remote(
                to_y.at[d - 1, rows(g)],
                from_y.at[d - 1, rows(g)],
                ys,
                sems.at[4 + pt.ny + g],
                pt.dev(pt.yat(d), pt.z, pt.c),
            ).start()
    sends.add(to_y, ys)
    arrived(pt, from_core.at[0], sems.at[4])
    if between is not None:
        between()
    for g in range(pt.parts):
        acc = mine(pt.y, g) + from_core[0, rows(g), :].astype(F32)
        arrived(pt, from_y.at[:, rows(g)], sems.at[4 + pt.ny + g])
        for d in pt.ydist:
            acc = acc + from_y[d - 1, rows(g), :].astype(F32)
        if finish is not None:
            acc = finish(acc, g)
        to_z[rows(g), :] = acc.astype(BF16)
        if g == last:
            total = acc[n - FEAT :, :]
        for j in range(g * pt.gs, (g + 1) * pt.gs):
            if j == pt.nz - 1:
                continue
            d = pt.dist[j]
            there = pt.slot_of[(pt.nz - d) % pt.nz]
            remote(
                to_z.at[pl.ds(j * FEAT, FEAT)], from_z.at[there], zs, zr, pt.dev(pt.y, pt.zat(d), pt.c)
            ).start()
    sends.flush()
    sends.add(to_z.at[pl.ds(0, (pt.nz - 1) * FEAT)], zs)
    arrived(pt, from_z.at[pl.ds(0, pt.nz - 1)], zr)
    for j in range(pt.nz - 1):
        total = total + from_z[j].astype(F32)
    return total


def kernel(heads, vocab, *refs):
    (hid_hbm, bias_hbm, tgt_hbm, msk_hbm, wres_hbm, wout_hbm, gh_out, gw_out, gb_out, loss_out) = refs[:10]
    (wo, wot, wr, wrt, buf1, buf2, flat1, flat2, logits, eo, prod, prod2, gw, st, st_y, sz, st_z, gx, gx_in) = refs[10:29]
    rs1, rs2 = refs[29:35], refs[35:41]
    t_to_core, t_from_core, t_mine, t_to_y, t_from_y = refs[41:46]
    ag1_s, ag2_s, rs1_s, rs2_s, t_s, tail_s, local = refs[46:53]
    bias, tgt, msk = refs[53:56]
    pt = Place(heads, vocab)
    ny, nz = pt.ny, pt.nz
    nrow = buf1.shape[-1]
    nvoc = wo.shape[0]
    feats = wo.shape[1]
    ychunk = feats // ny
    sends = Sends(pt)

    hid = buf1.at[pt.c, 0, nz - 1]
    get_wr = pltpu.make_async_copy(wres_hbm, wr, local.at[0])
    get_wo = pltpu.make_async_copy(wout_hbm, wo, local.at[1])
    get_hid = pltpu.make_async_copy(hid_hbm, hid, local.at[3])
    get_small = [
        pltpu.make_async_copy(src, dst, local.at[4 + k])
        for k, (src, dst) in enumerate(((bias_hbm, bias), (tgt_hbm, tgt), (msk_hbm, msk)))
    ]
    for cp in [get_hid, get_wr, *get_small, get_wo]:
        cp.start()

    peers = [pt.dev(pt.y, pt.zat(d), pt.c) for d in pt.dist[:-1]]
    plane = [(dy, dc) for dy in range(ny) for dc in range(2) if dy or dc]
    near = [pt.dev(pt.yat(dy), pt.z, lax.rem(pt.c + dc, 2)) for dy, dc in plane]
    xpeers = [(lax.rem(pt.x + d, heads), pt.v) for d in range(1, heads)]
    barrier = pltpu.get_barrier_semaphore()
    for dev in peers + near + xpeers:
        pl.semaphore_signal(barrier, inc=1, device_id=dev, device_id_type=MESH)

    per = 256 // (2 * FEAT)

    def place_rows(dst, chunk, i):
        y = lax.div(i * per, nz)
        z0 = lax.rem(i * per, nz)
        for k in range(per):
            j = pt.slot(z0 + k)
            for core in range(2):
                r = (k * 2 + core) * FEAT
                dst[core, y, j] = chunk[r : r + FEAT, :]

    def turn_wr(i, carry):
        place_rows(wrt, wr[:, pl.ds(pl.multiple_of(i * 256, 256), 256)].T, i)
        return carry

    for cp in get_small:
        cp.wait()
    get_hid.wait()
    pl.semaphore_wait(barrier, len(peers) + len(near) + len(xpeers))

    def turn_wo(i, carry):
        place_rows(wot, wo[:, pl.ds(pl.multiple_of(i * 256, 256), 256)].T, i)
        return carry

    def turn():
        get_wr.wait()
        lax.fori_loop(0, feats // 256, turn_wr, 0)
        get_wo.wait()
        lax.fori_loop(0, feats // 256, turn_wo, 0)

    gather(pt, buf1, ag1_s, sends, turn)
    in_order(pt, buf1, flat1)

    eye = lax.broadcasted_iota(jnp.int32, (FEAT, FEAT), 0) == lax.broadcasted_iota(jnp.int32, (FEAT, FEAT), 1)
    bias_col = jnp.sum(jnp.where(eye, bias[...], 0.0), axis=1, keepdims=True)
    pre = jnp.zeros((FEAT, nrow), F32)
    for y in range(ny):
        pre = pre + jnp.dot(
            wr[:, y * ychunk : (y + 1) * ychunk], flat1[y * ychunk : (y + 1) * ychunk, :], preferred_element_type=F32
        )
    pre = pre + bias_col
    sig = jax.nn.sigmoid(pre)
    buf2[pt.c, 0, nz - 1] = (hid[...].astype(F32) + pre * sig).astype(BF16)
    gate = sig * (1.0 + pre * (1.0 - sig))

    ids = pt.v * nvoc + lax.broadcasted_iota(jnp.int32, (nvoc, nrow), 0)
    hit = ids == tgt[...]

    def target_rows():
        sends.flush()
        eo[...] = hit.astype(BF16)

        def rows_of(core, y):
            w = wot[core, y].reshape(nz * FEAT, nvoc)
            return jnp.dot(w, eo[...], preferred_element_type=F32).astype(BF16)

        for d in range(ny):
            t_to_core[d] = rows_of(1 - pt.c, pt.yat(d))
        remote(t_to_core, t_from_core, t_s.at[0], t_s.at[1], pt.sib).start()
        for d in range(ny):
            t_mine[d] = rows_of(pt.c, pt.yat(d))
        arrived(pt, t_from_core, t_s.at[1])
        for d in pt.ydist:
            t_to_y[d - 1] = t_mine[d] + t_from_core[d]
            remote(t_to_y.at[d - 1], t_from_y.at[d - 1], t_s.at[2], t_s.at[3], pt.dev(pt.yat(d), pt.z, pt.c)).start()
        sends.add(t_to_core, t_s.at[0])
        sends.add(t_to_y, t_s.at[2])

    gather(pt, buf2, ag2_s, sends, target_rows)
    in_order(pt, buf2, flat2)

    logits[...] = jnp.zeros_like(logits)

    def logit_step(i, carry):
        at = pl.ds(pl.multiple_of(i * ychunk, ychunk), ychunk)
        logits[...] += jnp.dot(wo[:, at], flat2[at, :], preferred_element_type=F32)
        return carry

    lax.fori_loop(0, ny, logit_step, 0)
    lg = logits[...]
    top = jnp.max(lg, axis=0, keepdims=True)
    picked = jnp.sum(jnp.where(hit, lg, 0.0), axis=0, keepdims=True)
    e = jnp.exp(lg - top)
    e_hit = jnp.sum(jnp.where(hit, e, 0.0), axis=0, keepdims=True)
    e = jnp.where(hit, 0.0, e)
    rest = jnp.sum(e, axis=0, keepdims=True)
    eo[...] = e.astype(BF16)

    def pack(*values):
        r = lax.broadcasted_iota(jnp.int32, (8, nrow), 0)
        out = jnp.zeros((8, nrow), F32)
        for k, value in enumerate(values):
            out = jnp.where(r == k, value, out)
        return out

    def merge(ref, count):
        tops = [ref[i, 0:1, :] for i in range(count)]
        best = functools.reduce(jnp.maximum, tops)
        scale = [jnp.exp(t - best) for t in tops]
        others = sum(ref[i, 1:2, :] * scale[i] for i in range(count))
        target = sum(ref[i, 2:3, :] * scale[i] for i in range(count))
        pick = sum(ref[i, 3:4, :] for i in range(count))
        return best, others, target, pick

    packed = pack(top, rest, e_hit, picked)
    st[...] = packed
    me = pt.y * 2 + pt.c
    st_y[me] = packed
    for dev in near:
        remote(st, st_y.at[me], tail_s.at[0], tail_s.at[1], dev).start()

    def product(i, carry):
        core, y = lax.div(i, ny), lax.rem(i, ny)
        prod[core, y] = jnp.dot(wot[core, y].reshape(nz * FEAT, nvoc), eo[...], preferred_element_type=F32)
        return carry

    lax.fori_loop(0, 2 * ny, product, 0)
    arrived(pt, st_y.at[pl.ds(0, 2 * ny - 1)], tail_s.at[1])
    sends.add(st_y.at[pl.ds(0, 2 * ny - 1)], tail_s.at[0])
    plane_stats = merge(st_y, 2 * ny)
    plane_top = plane_stats[0]
    scale = jnp.exp(top - plane_top)
    n = pt.gs * FEAT

    def stats_out():
        packed = pack(*plane_stats)
        sz[...] = packed
        st_z[pt.z] = packed
        for d in pt.dist[:-1]:
            remote(sz, st_z.at[pt.z], tail_s.at[2], tail_s.at[3], pt.dev(pt.y, pt.zat(d), pt.c)).start()

    factors = []

    def stats_in():
        arrived(pt, st_z.at[pl.ds(0, nz - 1)], tail_s.at[3])
        sends.add(st_z.at[pl.ds(0, nz - 1)], tail_s.at[2])
        best, others, target, pick = merge(st_z, nz)
        total = others + target
        lse = best + jnp.log(total)
        factor = jnp.float32(0.8**heads)
        for k in range(heads - 1):
            factor = jnp.where(pt.x == k, jnp.float32(0.8 ** (k + 1)), factor)
        weight = factor * msk[...].astype(F32) / nrow
        loss_out[...] = jnp.sum(weight * (lse - pick), axis=1, keepdims=True)
        alpha = weight * jnp.exp(plane_top - lse)
        beta = (-weight * (others / total)).astype(BF16).astype(F32)
        factors.extend((alpha, beta))
        arrived(pt, t_from_y, t_s.at[3])

    def finish(acc, g):
        alpha, beta = factors
        at = pl.ds(g * n, n)
        rows = t_mine[0, at, :].astype(F32) + t_from_core[0, at, :].astype(F32)
        for d in pt.ydist:
            rows = rows + t_from_y[d - 1, at, :].astype(F32)
        return alpha * acc + beta * rows

    dh = scatter(
        pt,
        lambda y, g: scale * prod[1 - pt.c, y, g * n : (g + 1) * n, :],
        lambda y, g: scale * prod[pt.c, y, g * n : (g + 1) * n, :],
        rs1,
        rs1_s,
        sends,
        stats_out,
        stats_in,
        finish,
    )
    dpre = (dh * gate).astype(BF16)
    gb = jnp.sum(dpre.astype(F32), axis=1, keepdims=True)
    gb_out[...] = jnp.sum(jnp.where(eye, gb, 0.0), axis=0, keepdims=True)

    for core in range(2):
        for y in range(ny):
            prod2[core, y] = jnp.dot(
                wrt[core, y].reshape(nz * FEAT, FEAT), dpre, preferred_element_type=F32
            )
    put_gw = pltpu.make_async_copy(gw, gw_out, local.at[2])

    def weight_grad():
        def step(i, carry):
            at = pl.ds(pl.multiple_of(i * 256, 256), 256)
            gw[:, at] = lax.dot_general(
                dpre, flat1[at, :], (((1,), (1,)), ((), ())), preferred_element_type=F32
            )
            return carry

        lax.fori_loop(0, feats // 256, step, 0)
        put_gw.start()

    back = scatter(
        pt,
        lambda y, g: prod2[1 - pt.c, y, g * n : (g + 1) * n, :],
        lambda y, g: prod2[pt.c, y, g * n : (g + 1) * n, :],
        rs2,
        rs2_s,
        sends,
        between=weight_grad,
    )
    part = dh + back
    gx[...] = part
    gx_in[pt.x] = part
    for dev in xpeers:
        remote(gx, gx_in.at[pt.x], tail_s.at[4], tail_s.at[5], dev).start()
    sends.flush()
    put_gw.wait()
    if heads > 1:
        others = gx_in.at[pl.ds(0, heads - 1)]
        arrived(pt, others, tail_s.at[5])
        sends.add(others, tail_s.at[4])
    gh_out[...] = sum(gx_in[k] for k in range(heads))
    sends.flush()


def body(heads, vocab, hidden, res_weight, res_bias, out_weight, targets, loss_mask):
    ny, nz = GRID[vocab]
    rows = hidden.shape[0]
    nvoc, feats = out_weight.shape[1:]
    parts = min(PARTS, nz)
    dma = pltpu.SemaphoreType.DMA
    vm = pltpu.VMEM
    scatter_bufs = [
        vm((ny, nz * FEAT, rows), BF16),
        vm((ny, nz * FEAT, rows), BF16),
        vm((ny - 1, nz * FEAT, rows), BF16),
        vm((ny - 1, nz * FEAT, rows), BF16),
        vm((nz * FEAT, rows), BF16),
        vm((nz, FEAT, rows), BF16),
    ]
    in_vmem = pl.BlockSpec(memory_space=pltpu.VMEM)
    anywhere = pl.BlockSpec(memory_space=pl.ANY)
    gh, gw, gb, loss = pl.pallas_call(
        functools.partial(kernel, heads, vocab),
        out_shape=(
            jax.ShapeDtypeStruct((FEAT, rows), F32),
            jax.ShapeDtypeStruct((FEAT, feats), F32),
            jax.ShapeDtypeStruct((1, FEAT), F32),
            jax.ShapeDtypeStruct((1, 1), F32),
        ),
        in_specs=[anywhere] * 6,
        out_specs=(in_vmem, anywhere, in_vmem, in_vmem),
        scratch_shapes=[
            vm((nvoc, feats), BF16),
            vm((2, ny, nz, FEAT, nvoc), BF16),
            vm((FEAT, feats), BF16),
            vm((2, ny, nz, FEAT, FEAT), BF16),
            vm((2, ny, nz, FEAT, rows), BF16),
            vm((2, ny, nz, FEAT, rows), BF16),
            vm((feats, rows), BF16),
            vm((feats, rows), BF16),
            vm((nvoc, rows), F32),
            vm((nvoc, rows), BF16),
            vm((2, ny, nz * FEAT, rows), F32),
            vm((2, ny, nz * FEAT, rows), F32),
            vm((FEAT, feats), F32),
            vm((8, rows), F32),
            vm((2 * ny, 8, rows), F32),
            vm((8, rows), F32),
            vm((nz, 8, rows), F32),
            vm((FEAT, rows), F32),
            vm((heads, FEAT, rows), F32),
            *scatter_bufs,
            *scatter_bufs,
            vm((ny, nz * FEAT, rows), BF16),
            vm((ny, nz * FEAT, rows), BF16),
            vm((ny, nz * FEAT, rows), BF16),
            vm((ny - 1, nz * FEAT, rows), BF16),
            vm((ny - 1, nz * FEAT, rows), BF16),
            dma((8,)),
            dma((8,)),
            dma((4 + ny + parts,)),
            dma((4 + ny + parts,)),
            dma((4,)),
            dma((6,)),
            dma((7,)),
            vm((1, FEAT), F32),
            vm((1, rows), jnp.int32),
            vm((1, rows), jnp.int32),
        ],
        name="heads_backward",
        compiler_params=pltpu.CompilerParams(
            collective_id=0, has_side_effects=True, vmem_limit_bytes=60 << 20
        ),
    )(hidden.T, res_bias, targets, loss_mask, res_weight[0].T, out_weight[0])
    return gh.T, gw.T[None], gb, loss.reshape(1)


def solution(mesh):
    placed = (
        P(None, "vocab"),
        P("head", None, "vocab"),
        P("head", "vocab"),
        P("head", "vocab", None),
        P("head", None),
        P("head", None),
    )
    return jax.shard_map(
        functools.partial(body, mesh.shape["head"], mesh.shape["vocab"]),
        mesh=mesh,
        in_specs=placed,
        out_specs=(P(None, "vocab"), P("head", None, "vocab"), P("head", "vocab"), P("head")),
        check_vma=False,
    )
```

time: 116 us -> 100 us (0.86)
  Pallas kernels: 105 us -> 93.1 us
  local copies, waits for them, and re-layouts: 7.7 us -> 4.37 us
    pallas_call x1, Pallas kernels: 105 us -> 93.1 us  [body(): pl.pallas_call(functools.partial(kernel, heads, vocab), out_shape=(jax.Sh...]
    unnamed x15 -> x3, local copies, waits for them, and re-layouts: 7.7 us -> 4.37 us
where the time goes in v2:
time: 100 us; the launch traced here: 99.8 us
  Pallas kernels  93.1 us (93%)
  local copies, waits for them, and re-layouts  4.37 us (4%)
  between operations  2.38 us (2%)
    pallas_call x1, Pallas kernels, body(): pl.pallas_call(functools.partial(kernel, heads, vocab), out_shape=(jax.Sh...  93.1 us
    unnamed x3, local copies, waits for them, and re-layouts  4.37 us

profile of v2, /device:TPU:1, one launch (start us, length us, event | category | flops | bytes accessed | tf_op | source)
XLA Modules:
  0.0 99.8 jit_solution(2298177747881955949)
XLA Ops:
  0.6 93.1 %heads_backward.1 = (f32[32,128]{1,0:T(8,128)}, f32[32,4096]{1,0:T(8,128)}, f32[1,32]{1,0:T(1,128)}, f32[1,1]{1,0:T(1,128)}) custom-call(bf16[32,128]{1,0:T(8,128)(2,1)} %bitcast.14, f32[1,32]{1,0:T(1,128)} %refs_1_.1, s32[1,128]{1,0:T(1,128)} %refs_2_.1, s32[1,128]{1,0:T(1,128)} %refs_3_.1, bf16[32,4096]{1,0:T(8,128)(2,1)} %bitcast.12, ...), custom_call_target="tpu_custom_call" | custom-call | tf_op jit(solution)/shard_map/heads_backward/pallas_call | solution.py:449
  93.7 1.3 %copy.14 = f32[128,32]{0,1:T(8,128)} copy(f32[128,32]{0,1:T(8,128)} %bitcast.13) | data formatting | bytes 32768
  95.0 1.9 %copy.15 = f32[1,4096,32]{1,2,0:T(8,128)} copy(f32[1,4096,32]{1,2,0:T(8,128)} %bitcast.11) | data formatting | bytes 1048576
  96.9 1.2 %copy.16 = f32[1,32]{1,0:T(1,128)} copy(f32[1,32]{1,0:T(1,128)} %get-tuple-element.18) | data formatting | bytes 256

commit v3 on v2

--- a/solution.py
+++ b/solution.py
@@ -12,7 +12,6 @@
 GRID = {128: (4, 16), 16: (2, 4), 8: (2, 2)}
 FEAT = 32
 PARTS = 4
-NEAR = 8
 
 
 class Place:
@@ -31,13 +30,25 @@
         self.half = half
         self.parts = min(PARTS, self.nz)
         self.gs = self.nz // self.parts
-        self.near = min(NEAR, self.nz // 2)
+        self.reach = self.nz // 4
         self.sib = (self.x, v + 1 - 2 * self.c)
         self.ydist = sorted(range(1, self.ny), key=lambda d: (-min(d, self.ny - d), d))
 
     def slot(self, z_abs):
         d = lax.rem(z_abs - self.z + self.nz, self.nz)
         return jnp.where(d >= self.half, jnp.where(d == self.half, 0, 2 * (d - self.half)), 2 * (self.half - d) - 1)
+
+    def gather_slot(self, d):
+        r = self.reach
+        return jnp.where(
+            d == 0,
+            4 * r - 1,
+            jnp.where(
+                d <= r,
+                3 * r - 2 + d,
+                jnp.where(d < 2 * r, d - 1, jnp.where(d < 3 * r, 3 * r - 1 - d, 6 * r - 2 - d)),
+            ),
+        )
 
     def yat(self, d):
         return lax.rem(self.y + d + self.ny, self.ny)
@@ -77,32 +88,43 @@
     zs, ys, cs, cr = (sems.at[k] for k in range(4))
     own = pt.nz - 1
     c = pt.c
-    groups = ((pt.nz - pt.near, pt.nz), (0, pt.nz - pt.near))
-    for d in pt.dist[:-1]:
-        there = pt.slot_of[(pt.nz - d) % pt.nz]
-        g = 0 if there >= groups[0][0] else 1
-        remote(buf.at[c, 0, own], buf.at[c, 0, there], zs, sems.at[4 + g], pt.dev(pt.y, pt.zat(d), c)).start()
+    r = pt.reach
+    behind, ahead = 2 * r - 1, 3 * r - 1
+    groups = ((behind, pt.nz), (0, behind))
+    for i in reversed(range(r)):
+        for d, there, sem in ((i + 1, behind + i, 4), (-i - 1, ahead + i, 5)):
+            remote(buf.at[c, 0, own], buf.at[c, 0, there], zs, sems.at[sem], pt.dev(pt.y, pt.zat(d), c)).start()
     if between is not None:
         between()
+    for first, n, there, d, sem in ((behind, r, 0, r, 4), (ahead, r - 1, r, -r, 5)):
+        arrived(pt, buf.at[c, 0, pl.ds(first, r)], sems.at[sem])
+        if n:
+            remote(
+                buf.at[c, 0, pl.ds(first, n)],
+                buf.at[c, 0, pl.ds(there, n)],
+                zs,
+                sems.at[6],
+                pt.dev(pt.y, pt.zat(d), c),
+            ).start()
 
     def across(rows, lo, hi):
         part = buf.at[c, pl.ds(*rows), pl.ds(lo, hi - lo)]
         remote(part, part, cs, cr, pt.sib).start()
 
     for g, (lo, hi) in enumerate(groups):
-        n = hi - lo - (g == 0)
-        arrived(pt, buf.at[c, 0, pl.ds(lo, n)], sems.at[4 + g])
+        if g == 1:
+            arrived(pt, buf.at[c, 0, pl.ds(lo, hi - lo)], sems.at[6])
         for d in pt.ydist:
             remote(
                 buf.at[c, 0, pl.ds(lo, hi - lo)],
                 buf.at[c, d, pl.ds(lo, hi - lo)],
                 ys,
-                sems.at[6 + g],
+                sems.at[7 + g],
                 pt.dev(pt.yat(d), pt.z, c),
             ).start()
         across((0, 1), lo, hi)
     for g, (lo, hi) in enumerate(groups):
-        arrived(pt, buf.at[c, pl.ds(1, pt.ny - 1), pl.ds(lo, hi - lo)], sems.at[6 + g])
+        arrived(pt, buf.at[c, pl.ds(1, pt.ny - 1), pl.ds(lo, hi - lo)], sems.at[7 + g])
         across((1, pt.ny - 1), lo, hi)
     arrived(pt, buf.at[1 - c], cr)
     sends.add(buf.at[c, 0, pl.ds(0, own)], zs)
@@ -113,7 +135,7 @@
 def in_order(pt, buf, flat):
     def step(i, carry):
         y, z = lax.div(i, pt.nz), lax.rem(i, pt.nz)
-        j = pt.slot(z)
+        j = pt.gather_slot(lax.rem(z - pt.z + pt.nz, pt.nz))
         y = lax.rem(pt.y - y + pt.ny, pt.ny)
         for core in range(2):
             flat[pl.ds(pl.multiple_of((i * 2 + core) * FEAT, FEAT), FEAT), :] = buf[core, y, j]
@@ -122,7 +144,7 @@
     lax.fori_loop(0, pt.ny * pt.nz, step, 0, unroll=4)
 
 
-def scatter(pt, theirs, mine, bufs, sems, sends, beside=None, between=None, finish=None):
+def scatter(pt, theirs, mine, bufs, sems, sends, beside=None, between=None, finish=None, late=None):
     to_core, from_core, to_y, from_y, to_z, from_z = bufs
     cs, ys, zs, zr = (sems.at[k] for k in range(4))
     n = pt.gs * FEAT
@@ -131,14 +153,14 @@
     def rows(g):
         return pl.ds(g * n, n)
 
+    if beside is not None:
+        beside()
     for d in pt.ydist + [0]:
         for g in range(pt.parts):
             to_core[d, rows(g), :] = theirs(pt.yat(d), g).astype(BF16)
         remote(to_core.at[d], from_core.at[d], cs, sems.at[4 + d], pt.sib).start()
     sends.flush()
     sends.add(to_core, cs)
-    if beside is not None:
-        beside()
     for g in range(pt.parts):
         for d in pt.ydist:
             if g == 0:
@@ -174,6 +196,8 @@
                 to_z.at[pl.ds(j * FEAT, FEAT)], from_z.at[there], zs, zr, pt.dev(pt.y, pt.zat(d), pt.c)
             ).start()
     sends.flush()
+    if late is not None:
+        late()
     sends.add(to_z.at[pl.ds(0, (pt.nz - 1) * FEAT)], zs)
     arrived(pt, from_z.at[pl.ds(0, pt.nz - 1)], zr)
     for j in range(pt.nz - 1):
@@ -207,7 +231,7 @@
     for cp in [get_hid, get_wr, *get_small, get_wo]:
         cp.start()
 
-    peers = [pt.dev(pt.y, pt.zat(d), pt.c) for d in pt.dist[:-1]]
+    peers = [pt.dev(pt.y, pt.zat(d), pt.c) for k in range(pt.reach, 0, -1) for d in (k, -k)]
     plane = [(dy, dc) for dy in range(ny) for dc in range(2) if dy or dc]
     near = [pt.dev(pt.yat(dy), pt.z, lax.rem(pt.c + dc, 2)) for dy, dc in plane]
     xpeers = [(lax.rem(pt.x + d, heads), pt.v) for d in range(1, heads)]
@@ -245,7 +269,23 @@
         get_wo.wait()
         lax.fori_loop(0, feats // 256, turn_wo, 0)
 
-    gather(pt, buf1, ag1_s, sends, turn)
+    ids = pt.v * nvoc + lax.broadcasted_iota(jnp.int32, (nvoc, nrow), 0)
+
+    def rows_of(core, y):
+        w = wot[core, y].reshape(nz * FEAT, nvoc)
+        return jnp.dot(w, eo[...], preferred_element_type=F32).astype(BF16)
+
+    def prepare():
+        turn()
+        eo[...] = (ids == tgt[...]).astype(BF16)
+        for d in range(ny):
+            t_to_core[d] = rows_of(1 - pt.c, pt.yat(d))
+        remote(t_to_core, t_from_core, t_s.at[0], t_s.at[1], pt.sib).start()
+        sends.add(t_to_core, t_s.at[0])
+        for d in range(ny):
+            t_mine[d] = rows_of(pt.c, pt.yat(d))
+
+    gather(pt, buf1, ag1_s, sends, prepare)
     in_order(pt, buf1, flat1)
 
     eye = lax.broadcasted_iota(jnp.int32, (FEAT, FEAT), 0) == lax.broadcasted_iota(jnp.int32, (FEAT, FEAT), 1)
@@ -260,27 +300,13 @@
     buf2[pt.c, 0, nz - 1] = (hid[...].astype(F32) + pre * sig).astype(BF16)
     gate = sig * (1.0 + pre * (1.0 - sig))
 
-    ids = pt.v * nvoc + lax.broadcasted_iota(jnp.int32, (nvoc, nrow), 0)
-    hit = ids == tgt[...]
 
     def target_rows():
-        sends.flush()
-        eo[...] = hit.astype(BF16)
-
-        def rows_of(core, y):
-            w = wot[core, y].reshape(nz * FEAT, nvoc)
-            return jnp.dot(w, eo[...], preferred_element_type=F32).astype(BF16)
-
-        for d in range(ny):
-            t_to_core[d] = rows_of(1 - pt.c, pt.yat(d))
-        remote(t_to_core, t_from_core, t_s.at[0], t_s.at[1], pt.sib).start()
-        for d in range(ny):
-            t_mine[d] = rows_of(pt.c, pt.yat(d))
         arrived(pt, t_from_core, t_s.at[1])
         for d in pt.ydist:
             t_to_y[d - 1] = t_mine[d] + t_from_core[d]
             remote(t_to_y.at[d - 1], t_from_y.at[d - 1], t_s.at[2], t_s.at[3], pt.dev(pt.yat(d), pt.z, pt.c)).start()
-        sends.add(t_to_core, t_s.at[0])
+        sends.flush()
         sends.add(t_to_y, t_s.at[2])
 
     gather(pt, buf2, ag2_s, sends, target_rows)
@@ -294,6 +320,7 @@
         return carry
 
     lax.fori_loop(0, ny, logit_step, 0)
+    hit = ids == tgt[...]
     lg = logits[...]
     top = jnp.max(lg, axis=0, keepdims=True)
     picked = jnp.sum(jnp.where(hit, lg, 0.0), axis=0, keepdims=True)
@@ -412,7 +439,7 @@
         rs2,
         rs2_s,
         sends,
-        between=weight_grad,
+        late=weight_grad,
     )
     part = dh + back
     gx[...] = part
@@ -483,8 +510,8 @@
             vm((ny, nz * FEAT, rows), BF16),
             vm((ny - 1, nz * FEAT, rows), BF16),
             vm((ny - 1, nz * FEAT, rows), BF16),
-            dma((8,)),
-            dma((8,)),
+            dma((9,)),
+            dma((9,)),
             dma((4 + ny + parts,)),
             dma((4 + ny + parts,)),
             dma((4,)),

time: 100 us -> 96.2 us (0.962)
  Pallas kernels: 93.1 us -> 89.2 us
    pallas_call x1, Pallas kernels: 93.1 us -> 89.2 us  [body(): pl.pallas_call(functools.partial(kernel, heads, vocab), out_shape=(jax.Sh...]
where the time goes in v3:
time: 96.2 us; the launch traced here: 96 us
  Pallas kernels  89.2 us (93%)
  local copies, waits for them, and re-layouts  4.37 us (5%)
  between operations  2.38 us (2%)
    pallas_call x1, Pallas kernels, body(): pl.pallas_call(functools.partial(kernel, heads, vocab), out_shape=(jax.Sh...  89.2 us
    unnamed x3, local copies, waits for them, and re-layouts  4.37 us

profile of v3, /device:TPU:1, one launch (start us, length us, event | category | flops | bytes accessed | tf_op | source)
XLA Modules:
  0.0 96.0 jit_solution(3041400750892927493)
XLA Ops:
  0.6 89.2 %heads_backward.1 = (f32[32,128]{1,0:T(8,128)}, f32[32,4096]{1,0:T(8,128)}, f32[1,32]{1,0:T(1,128)}, f32[1,1]{1,0:T(1,128)}) custom-call(bf16[32,128]{1,0:T(8,128)(2,1)} %bitcast.14, f32[1,32]{1,0:T(1,128)} %refs_1_.1, s32[1,128]{1,0:T(1,128)} %refs_2_.1, s32[1,128]{1,0:T(1,128)} %refs_3_.1, bf16[32,4096]{1,0:T(8,128)(2,1)} %bitcast.12, ...), custom_call_target="tpu_custom_call" | custom-call | tf_op jit(solution)/shard_map/heads_backward/pallas_call | solution.py:476
  89.9 1.3 %copy.14 = f32[128,32]{0,1:T(8,128)} copy(f32[128,32]{0,1:T(8,128)} %bitcast.13) | data formatting | bytes 32768
  91.2 1.9 %copy.15 = f32[1,4096,32]{1,2,0:T(8,128)} copy(f32[1,4096,32]{1,2,0:T(8,128)} %bitcast.11) | data formatting | bytes 1048576
  93.0 1.2 %copy.16 = f32[1,32]{1,0:T(1,128)} copy(f32[1,32]{1,0:T(1,128)} %get-tuple-element.18) | data formatting | bytes 256

commit v4 on v3

--- a/solution.py
+++ b/solution.py
@@ -11,7 +11,7 @@
 F32, BF16 = jnp.float32, jnp.bfloat16
 GRID = {128: (4, 16), 16: (2, 4), 8: (2, 2)}
 FEAT = 32
-PARTS = 4
+PARTS = 8
 
 
 class Place:
@@ -84,7 +84,7 @@
     remote(ref, ref, sem, sem, pt.sib).wait_recv()
 
 
-def gather(pt, buf, sems, sends, between=None):
+def gather(pt, buf, sems, sends, between=None, late=None):
     zs, ys, cs, cr = (sems.at[k] for k in range(4))
     own = pt.nz - 1
     c = pt.c
@@ -126,6 +126,8 @@
     for g, (lo, hi) in enumerate(groups):
         arrived(pt, buf.at[c, pl.ds(1, pt.ny - 1), pl.ds(lo, hi - lo)], sems.at[7 + g])
         across((1, pt.ny - 1), lo, hi)
+        if g == 0 and late is not None:
+            late()
     arrived(pt, buf.at[1 - c], cr)
     sends.add(buf.at[c, 0, pl.ds(0, own)], zs)
     sends.add(buf.at[c, pl.ds(1, pt.ny - 1)], ys)
@@ -144,7 +146,15 @@
     lax.fori_loop(0, pt.ny * pt.nz, step, 0, unroll=4)
 
 
-def scatter(pt, theirs, mine, bufs, sems, sends, beside=None, between=None, finish=None, late=None):
+def send_along_z(pt, src, dst, j, send, recv):
+    d = pt.dist[j]
+    there = pt.slot_of[(pt.nz - d) % pt.nz]
+    remote(
+        src.at[pl.ds(j * FEAT, FEAT)], dst.at[there], send, recv, pt.dev(pt.y, pt.zat(d), pt.c)
+    ).start()
+
+
+def scatter(pt, term, own, bufs, sems, sends, ready=None, beside=None, late=None, combine=None):
     to_core, from_core, to_y, from_y, to_z, from_z = bufs
     cs, ys, zs, zr = (sems.at[k] for k in range(4))
     n = pt.gs * FEAT
@@ -153,19 +163,24 @@
     def rows(g):
         return pl.ds(g * n, n)
 
-    if beside is not None:
-        beside()
     for d in pt.ydist + [0]:
-        for g in range(pt.parts):
-            to_core[d, rows(g), :] = theirs(pt.yat(d), g).astype(BF16)
+        to_core[d] = term(1 - pt.c, pt.yat(d)).astype(BF16)
         remote(to_core.at[d], from_core.at[d], cs, sems.at[4 + d], pt.sib).start()
+    for d in pt.ydist + [0]:
+        own[d] = term(pt.c, pt.yat(d))
     sends.flush()
     sends.add(to_core, cs)
+    factors = ready() if ready is not None else None
+
+    def both(d, g):
+        mine, other = own[d, rows(g), :], from_core[d, rows(g), :].astype(F32)
+        return mine + other if factors is None else factors[0] * mine + factors[1] * other
+
     for g in range(pt.parts):
         for d in pt.ydist:
             if g == 0:
                 arrived(pt, from_core.at[d], sems.at[4 + d])
-            to_y[d - 1, rows(g), :] = (mine(pt.yat(d), g) + from_core[d, rows(g), :].astype(F32)).astype(BF16)
+            to_y[d - 1, rows(g), :] = both(d, g).astype(BF16)
             remote(
                 to_y.at[d - 1, rows(g)],
                 from_y.at[d - 1, rows(g)],
@@ -175,43 +190,34 @@
             ).start()
     sends.add(to_y, ys)
     arrived(pt, from_core.at[0], sems.at[4])
-    if between is not None:
-        between()
+    if beside is not None:
+        beside()
     for g in range(pt.parts):
-        acc = mine(pt.y, g) + from_core[0, rows(g), :].astype(F32)
+        acc = both(0, g)
         arrived(pt, from_y.at[:, rows(g)], sems.at[4 + pt.ny + g])
         for d in pt.ydist:
             acc = acc + from_y[d - 1, rows(g), :].astype(F32)
-        if finish is not None:
-            acc = finish(acc, g)
         to_z[rows(g), :] = acc.astype(BF16)
         if g == last:
             total = acc[n - FEAT :, :]
-        for j in range(g * pt.gs, (g + 1) * pt.gs):
-            if j == pt.nz - 1:
-                continue
-            d = pt.dist[j]
-            there = pt.slot_of[(pt.nz - d) % pt.nz]
-            remote(
-                to_z.at[pl.ds(j * FEAT, FEAT)], from_z.at[there], zs, zr, pt.dev(pt.y, pt.zat(d), pt.c)
-            ).start()
+        for j in range(g * pt.gs, min((g + 1) * pt.gs, pt.nz - 1)):
+            send_along_z(pt, to_z, from_z, j, zs, zr)
     sends.flush()
     if late is not None:
         late()
     sends.add(to_z.at[pl.ds(0, (pt.nz - 1) * FEAT)], zs)
     arrived(pt, from_z.at[pl.ds(0, pt.nz - 1)], zr)
-    for j in range(pt.nz - 1):
-        total = total + from_z[j].astype(F32)
-    return total
+    others = [from_z[j].astype(F32) for j in range(pt.nz - 1)]
+    return sum(others, total) if combine is None else combine(total, others)
 
 
 def kernel(heads, vocab, *refs):
     (hid_hbm, bias_hbm, tgt_hbm, msk_hbm, wres_hbm, wout_hbm, gh_out, gw_out, gb_out, loss_out) = refs[:10]
-    (wo, wot, wr, wrt, buf1, buf2, flat1, flat2, logits, eo, prod, prod2, gw, st, st_y, sz, st_z, gx, gx_in) = refs[10:29]
+    (wo, wot, wr, wrt, buf1, buf2, flat1, flat2, logits, eo, hits, own, gw, st, st_y, sz, st_z, gx, gx_in) = refs[10:29]
     rs1, rs2 = refs[29:35], refs[35:41]
-    t_to_core, t_from_core, t_mine, t_to_y, t_from_y = refs[41:46]
-    ag1_s, ag2_s, rs1_s, rs2_s, t_s, tail_s, local = refs[46:53]
-    bias, tgt, msk = refs[53:56]
+    t_to_core, t_from_core, t_mine, t_to_y, t_from_y, t_to_z, t_from_z = refs[41:48]
+    ag1_s, ag2_s, rs1_s, rs2_s, t_s, tail_s, local = refs[48:55]
+    bias, tgt, msk = refs[55:58]
     pt = Place(heads, vocab)
     ny, nz = pt.ny, pt.nz
     nrow = buf1.shape[-1]
@@ -273,11 +279,10 @@
 
     def rows_of(core, y):
         w = wot[core, y].reshape(nz * FEAT, nvoc)
-        return jnp.dot(w, eo[...], preferred_element_type=F32).astype(BF16)
+        return jnp.dot(w, hits[...], preferred_element_type=F32).astype(BF16)
 
     def prepare():
-        turn()
-        eo[...] = (ids == tgt[...]).astype(BF16)
+        hits[...] = (ids == tgt[...]).astype(BF16)
         for d in range(ny):
             t_to_core[d] = rows_of(1 - pt.c, pt.yat(d))
         remote(t_to_core, t_from_core, t_s.at[0], t_s.at[1], pt.sib).start()
@@ -285,7 +290,7 @@
         for d in range(ny):
             t_mine[d] = rows_of(pt.c, pt.yat(d))
 
-    gather(pt, buf1, ag1_s, sends, prepare)
+    gather(pt, buf1, ag1_s, sends, turn, prepare)
     in_order(pt, buf1, flat1)
 
     eye = lax.broadcasted_iota(jnp.int32, (FEAT, FEAT), 0) == lax.broadcasted_iota(jnp.int32, (FEAT, FEAT), 1)
@@ -309,7 +314,17 @@
         sends.flush()
         sends.add(t_to_y, t_s.at[2])
 
-    gather(pt, buf2, ag2_s, sends, target_rows)
+    def target_rows_z():
+        arrived(pt, t_from_y, t_s.at[3])
+        rows = t_mine[0] + t_from_core[0]
+        for d in pt.ydist:
+            rows = rows + t_from_y[d - 1]
+        t_to_z[...] = rows
+        for j in range(nz - 1):
+            send_along_z(pt, t_to_z, t_from_z, j, t_s.at[4], t_s.at[5])
+        sends.add(t_to_z.at[pl.ds(0, (nz - 1) * FEAT)], t_s.at[4])
+
+    gather(pt, buf2, ag2_s, sends, target_rows, target_rows_z)
     in_order(pt, buf2, flat2)
 
     logits[...] = jnp.zeros_like(logits)
@@ -353,18 +368,13 @@
     for dev in near:
         remote(st, st_y.at[me], tail_s.at[0], tail_s.at[1], dev).start()
 
-    def product(i, carry):
-        core, y = lax.div(i, ny), lax.rem(i, ny)
-        prod[core, y] = jnp.dot(wot[core, y].reshape(nz * FEAT, nvoc), eo[...], preferred_element_type=F32)
-        return carry
-
-    lax.fori_loop(0, 2 * ny, product, 0)
-    arrived(pt, st_y.at[pl.ds(0, 2 * ny - 1)], tail_s.at[1])
-    sends.add(st_y.at[pl.ds(0, 2 * ny - 1)], tail_s.at[0])
-    plane_stats = merge(st_y, 2 * ny)
-    plane_top = plane_stats[0]
-    scale = jnp.exp(top - plane_top)
-    n = pt.gs * FEAT
+    plane_stats = []
+
+    def stats_near():
+        arrived(pt, st_y.at[pl.ds(0, 2 * ny - 1)], tail_s.at[1])
+        sends.add(st_y.at[pl.ds(0, 2 * ny - 1)], tail_s.at[0])
+        plane_stats.extend(merge(st_y, 2 * ny))
+        return jnp.exp(top - plane_stats[0]), jnp.exp(st_y[me + 1 - 2 * pt.c, 0:1, :] - plane_stats[0])
 
     def stats_out():
         packed = pack(*plane_stats)
@@ -373,52 +383,34 @@
         for d in pt.dist[:-1]:
             remote(sz, st_z.at[pt.z], tail_s.at[2], tail_s.at[3], pt.dev(pt.y, pt.zat(d), pt.c)).start()
 
-    factors = []
-
-    def stats_in():
+    def weigh(mine, others):
         arrived(pt, st_z.at[pl.ds(0, nz - 1)], tail_s.at[3])
         sends.add(st_z.at[pl.ds(0, nz - 1)], tail_s.at[2])
-        best, others, target, pick = merge(st_z, nz)
-        total = others + target
+        best, rest, target, pick = merge(st_z, nz)
+        total = rest + target
         lse = best + jnp.log(total)
         factor = jnp.float32(0.8**heads)
         for k in range(heads - 1):
             factor = jnp.where(pt.x == k, jnp.float32(0.8 ** (k + 1)), factor)
         weight = factor * msk[...].astype(F32) / nrow
         loss_out[...] = jnp.sum(weight * (lse - pick), axis=1, keepdims=True)
-        alpha = weight * jnp.exp(plane_top - lse)
-        beta = (-weight * (others / total)).astype(BF16).astype(F32)
-        factors.extend((alpha, beta))
-        arrived(pt, t_from_y, t_s.at[3])
-
-    def finish(acc, g):
-        alpha, beta = factors
-        at = pl.ds(g * n, n)
-        rows = t_mine[0, at, :].astype(F32) + t_from_core[0, at, :].astype(F32)
-        for d in pt.ydist:
-            rows = rows + t_from_y[d - 1, at, :].astype(F32)
-        return alpha * acc + beta * rows
-
-    dh = scatter(
-        pt,
-        lambda y, g: scale * prod[1 - pt.c, y, g * n : (g + 1) * n, :],
-        lambda y, g: scale * prod[pt.c, y, g * n : (g + 1) * n, :],
-        rs1,
-        rs1_s,
-        sends,
-        stats_out,
-        stats_in,
-        finish,
-    )
+        beta = (-weight * (rest / total)).astype(BF16).astype(F32)
+        arrived(pt, t_from_z.at[pl.ds(0, nz - 1)], t_s.at[5])
+        rows = t_to_z[(nz - 1) * FEAT :, :].astype(F32)
+        out = jnp.exp(plane_stats[0] - lse) * mine
+        for j in range(nz - 1):
+            rows = rows + t_from_z[j].astype(F32)
+            out = out + jnp.exp(st_z[pt.zat(pt.dist[j]), 0:1, :] - lse) * others[j]
+        return weight * out + beta * rows
+
+    def vocab_term(core, y):
+        return jnp.dot(wot[core, y].reshape(nz * FEAT, nvoc), eo[...], preferred_element_type=F32)
+
+    dh = scatter(pt, vocab_term, own, rs1, rs1_s, sends, stats_near, stats_out, None, weigh)
     dpre = (dh * gate).astype(BF16)
     gb = jnp.sum(dpre.astype(F32), axis=1, keepdims=True)
     gb_out[...] = jnp.sum(jnp.where(eye, gb, 0.0), axis=0, keepdims=True)
 
-    for core in range(2):
-        for y in range(ny):
-            prod2[core, y] = jnp.dot(
-                wrt[core, y].reshape(nz * FEAT, FEAT), dpre, preferred_element_type=F32
-            )
     put_gw = pltpu.make_async_copy(gw, gw_out, local.at[2])
 
     def weight_grad():
@@ -432,15 +424,10 @@
         lax.fori_loop(0, feats // 256, step, 0)
         put_gw.start()
 
-    back = scatter(
-        pt,
-        lambda y, g: prod2[1 - pt.c, y, g * n : (g + 1) * n, :],
-        lambda y, g: prod2[pt.c, y, g * n : (g + 1) * n, :],
-        rs2,
-        rs2_s,
-        sends,
-        late=weight_grad,
-    )
+    def residual_term(core, y):
+        return jnp.dot(wrt[core, y].reshape(nz * FEAT, FEAT), dpre, preferred_element_type=F32)
+
+    back = scatter(pt, residual_term, own, rs2, rs2_s, sends, late=weight_grad)
     part = dh + back
     gx[...] = part
     gx_in[pt.x] = part
@@ -494,8 +481,8 @@
             vm((feats, rows), BF16),
             vm((nvoc, rows), F32),
             vm((nvoc, rows), BF16),
-            vm((2, ny, nz * FEAT, rows), F32),
-            vm((2, ny, nz * FEAT, rows), F32),
+            vm((nvoc, rows), BF16),
+            vm((ny, nz * FEAT, rows), F32),
             vm((FEAT, feats), F32),
             vm((8, rows), F32),
             vm((2 * ny, 8, rows), F32),
@@ -510,11 +497,13 @@
             vm((ny, nz * FEAT, rows), BF16),
             vm((ny - 1, nz * FEAT, rows), BF16),
             vm((ny - 1, nz * FEAT, rows), BF16),
+            vm((nz * FEAT, rows), BF16),
+            vm((nz, FEAT, rows), BF16),
             dma((9,)),
             dma((9,)),
             dma((4 + ny + parts,)),
             dma((4 + ny + parts,)),
-            dma((4,)),
+            dma((6,)),
             dma((6,)),
             dma((7,)),
             vm((1, FEAT), F32),

time: 96.2 us -> 91.6 us (0.952)
  Pallas kernels: 89.2 us -> 84.6 us
    pallas_call x1, Pallas kernels: 89.2 us -> 84.6 us  [body(): pl.pallas_call(functools.partial(kernel, heads, vocab), out_shape=(jax.Sh...]
where the time goes in v4:
time: 91.6 us; the launch traced here: 91.4 us
  Pallas kernels  84.6 us (92%)
  local copies, waits for them, and re-layouts  4.37 us (5%)
  between operations  2.38 us (3%)
    pallas_call x1, Pallas kernels, body(): pl.pallas_call(functools.partial(kernel, heads, vocab), out_shape=(jax.Sh...  84.6 us
    unnamed x3, local copies, waits for them, and re-layouts  4.37 us

profile of v4, /device:TPU:1, one launch (start us, length us, event | category | flops | bytes accessed | tf_op | source)
XLA Modules:
  0.0 91.4 jit_solution(4205511140557282185)
XLA Ops:
  0.6 84.6 %heads_backward.1 = (f32[32,128]{1,0:T(8,128)}, f32[32,4096]{1,0:T(8,128)}, f32[1,32]{1,0:T(1,128)}, f32[1,1]{1,0:T(1,128)}) custom-call(bf16[32,128]{1,0:T(8,128)(2,1)} %bitcast.14, f32[1,32]{1,0:T(1,128)} %refs_1_.1, s32[1,128]{1,0:T(1,128)} %refs_2_.1, s32[1,128]{1,0:T(1,128)} %refs_3_.1, bf16[32,4096]{1,0:T(8,128)(2,1)} %bitcast.12, ...), custom_call_target="tpu_custom_call" | custom-call | tf_op jit(solution)/shard_map/heads_backward/pallas_call | solution.py:463
  85.3 1.3 %copy.14 = f32[128,32]{0,1:T(8,128)} copy(f32[128,32]{0,1:T(8,128)} %bitcast.13) | data formatting | bytes 32768
  86.6 1.9 %copy.15 = f32[1,4096,32]{1,2,0:T(8,128)} copy(f32[1,4096,32]{1,2,0:T(8,128)} %bitcast.11) | data formatting | bytes 1048576
  88.5 1.2 %copy.16 = f32[1,32]{1,0:T(1,128)} copy(f32[1,32]{1,0:T(1,128)} %get-tuple-element.18) | data formatting | bytes 256

commit v5 on v4

--- a/solution.py
+++ b/solution.py
@@ -463,13 +463,13 @@
     gh, gw, gb, loss = pl.pallas_call(
         functools.partial(kernel, heads, vocab),
         out_shape=(
-            jax.ShapeDtypeStruct((FEAT, rows), F32),
-            jax.ShapeDtypeStruct((FEAT, feats), F32),
-            jax.ShapeDtypeStruct((1, FEAT), F32),
+            vm((FEAT, rows), F32),
+            vm((FEAT, feats), F32),
+            vm((1, FEAT), F32),
             jax.ShapeDtypeStruct((1, 1), F32),
         ),
         in_specs=[anywhere] * 6,
-        out_specs=(in_vmem, anywhere, in_vmem, in_vmem),
+        out_specs=(in_vmem, in_vmem, in_vmem, in_vmem),
         scratch_shapes=[
             vm((nvoc, feats), BF16),
             vm((2, ny, nz, FEAT, nvoc), BF16),

time: 91.6 us -> 88.7 us (0.968)
  local copies, waits for them, and re-layouts: 4.37 us -> 1.91 us
    unnamed x3, local copies, waits for them, and re-layouts: 4.37 us -> 1.91 us
where the time goes in v5:
time: 88.7 us; the launch traced here: 88.6 us
  Pallas kernels  84.3 us (95%)
  between operations  2.33 us (3%)
  local copies, waits for them, and re-layouts  1.91 us (2%)
    pallas_call x1, Pallas kernels, body(): pl.pallas_call(functools.partial(kernel, heads, vocab), out_shape=(vm((FE...  84.3 us
    unnamed x3, local copies, waits for them, and re-layouts  1.91 us

profile of v5, /device:TPU:1, one launch (start us, length us, event | category | flops | bytes accessed | tf_op | source)
XLA Modules:
  0.0 88.6 jit_solution(16428952986431818115)
XLA Ops:
  0.6 84.3 %heads_backward.1 = (f32[32,128]{1,0:T(8,128)S(1)}, f32[32,4096]{1,0:T(8,128)S(1)}, f32[1,32]{1,0:T(1,128)S(1)}, f32[1,1]{1,0:T(1,128)}) custom-call(bf16[32,128]{1,0:T(8,128)(2,1)} %bitcast.14, f32[1,32]{1,0:T(1,128)} %refs_1_.1, s32[1,128]{1,0:T(1,128)} %refs_2_.1, s32[1,128]{1,0:T(1,128)} %refs_3_.1, bf16[32,4096]{1,0:T(8,128)(2,1)} %bitcast.13, ...), custom_call_target="tpu_custom_call" | custom-call | tf_op jit(solution)/shard_map/heads_backward/pallas_call | solution.py:463
  85.0 0.6 copy.14
  85.6 0.8 copy.15
  86.4 0.5 copy.16
